TPU v7x, 32 devices: a whole 2x2x4 slice. The times are simulated.
32 devices in a mesh: row: 4 (over x, core), col: 8 (over z, y).
Axes of the slice: x: 2, y: 2, z: 4, core: 2. Of those that a mesh axis runs over, the one named last changes fastest.
Arguments:
- tokens: bfloat16 [128, 8192], P('col', 'row'), may hold values from -6 to 6
- out_grad: bfloat16 [128, 8192], P('col', 'row'), may hold values from -2 to 2
- gate_weight: bfloat16 [8192, 28672], P('row', 'col'), may hold values from -0.0625 to 0.0625
- up_weight: bfloat16 [8192, 28672], P('row', 'col'), may hold values from -0.0625 to 0.0625
- down_weight: bfloat16 [28672, 8192], P('col', 'row'), may hold values from -0.03125 to 0.03125
Outputs:
- grad_input: bfloat16 [128, 8192], P('col', 'row')
- grad_gate: bfloat16 [8192, 28672], P('row', 'col')
- grad_up: bfloat16 [8192, 28672], P('row', 'col')
- grad_down: bfloat16 [28672, 8192], P('col', 'row')
All inputs are finite; a program needn't handle non-finite values.
Results may differ from a plain program's by a relative error of at most 0.005.
Values may be sent and summed in bfloat16 or wider, within the bound.
A program may use at most 128 MiB of HBM per device.

v0:
```python
import jax
import jax.numpy as jnp
from jax import lax
from jax.sharding import PartitionSpec as P


def pointwise(gate, up, hidden_grad):
    logistic = jax.nn.sigmoid(gate)
    active = gate * logistic
    hidden = (active * up).astype(jnp.bfloat16)
    d_gate = (hidden_grad * up * logistic * (1.0 + gate * (1.0 - logistic))).astype(jnp.bfloat16)
    d_up = (hidden_grad * active).astype(jnp.bfloat16)
    return (hidden, d_gate, d_up)


def contract_last(left, right):
    return lax.dot_general(
        left, right, (((1,), (1,)), ((), ())), preferred_element_type=jnp.float32
    )


def contract_first(left, right):
    return lax.dot_general(
        left, right, (((0,), (0,)), ((), ())), preferred_element_type=jnp.float32
    )


def local(tokens, out_grad, gate_weight, up_weight, down_weight):
    full_tokens, full_grad = (
        lax.all_gather(tokens, "col", axis=0, tiled=True),
        lax.all_gather(out_grad, "col", axis=0, tiled=True),
    )
    gate_part = jnp.dot(full_tokens, gate_weight, preferred_element_type=jnp.float32)
    up_part = jnp.dot(full_tokens, up_weight, preferred_element_type=jnp.float32)
    hidden_part = contract_last(full_grad, down_weight)
    gate, up, hidden_grad = lax.psum((gate_part, up_part, hidden_part), "row")
    hidden, d_gate, d_up = pointwise(gate, up, hidden_grad)
    grad_down = contract_first(hidden, full_grad).astype(jnp.bfloat16)
    grad_gate = contract_first(full_tokens, d_gate).astype(jnp.bfloat16)
    grad_up = contract_first(full_tokens, d_up).astype(jnp.bfloat16)
    grad_input = lax.psum_scatter(
        contract_last(d_gate, gate_weight) + contract_last(d_up, up_weight),
        "col",
        scatter_dimension=0,
        tiled=True,
    ).astype(jnp.bfloat16)
    return (grad_input, grad_gate, grad_up, grad_down)


def solution(mesh):
    in_specs = (P("col", "row"), P("col", "row"), P("row", "col"), P("row", "col"), P("col", "row"))
    out_specs = (P("col", "row"), P("row", "col"), P("row", "col"), P("col", "row"))
    return jax.shard_map(local, mesh=mesh, in_specs=in_specs, out_specs=out_specs, check_vma=False)
```

profile of v0, /device:TPU:0, one launch (start us, length us, event | category | flops | bytes accessed | tf_op | source)
XLA Modules:
  0.0 309.4 jit_solution(5140801094091039847)
XLA Ops:
  7.2 0.0 all-reduce.3.cloned.1.call-start
  7.2 33.2 %all_gather.7 = bf16[128,2048]{1,0:T(8,128)(2,1)S(1)} all-gather(bf16[16,2048]{1,0:T(8,128)(2,1)} %param.5), channel_id=1, replica_groups=mesh['row'=4,'col'=8] {'col'}, dimensions={0}, use_global_device_ids=true | all-gather | bytes 589824 | tf_op jit(solution)/shard_map/all_gather | solution.py:30
  40.4 31.4 %all_gather.6 = bf16[128,2048]{1,0:T(8,128)(2,1)S(1)} all-gather(bf16[16,2048]{1,0:T(8,128)(2,1)} %param.6), channel_id=1, replica_groups=mesh['row'=4,'col'=8] {'col'}, dimensions={0}, use_global_device_ids=true | all-gather | bytes 589824 | tf_op jit(solution)/shard_map/all_gather | solution.py:31
  71.8 0.0 copy-start
  71.8 8.6 %fusion.7 = f32[128,3584]{1,0:T(8,128)} fusion(bf16[128,2048]{1,0:T(8,128)(2,1)S(1)} %all_gather.7, bf16[2048,3584]{1,0:T(8,128)(2,1)} %param.7), kind=kOutput, calls=%fused_computation.14 | convolution fusion | flops 1879048192 | bytes 17039360 | tf_op jit(solution)/shard_map/dot_general | solution.py:33
  80.5 1.4 copy-done
  81.8 3.4 %fusion.6 = f32[128,3584]{1,0:T(8,128)} fusion(bf16[128,2048]{1,0:T(8,128)(2,1)S(1)} %all_gather.7, bf16[2048,3584]{1,0:T(8,128)(2,1)S(1)} %copy-done), kind=kOutput, calls=%fused_computation.13 | convolution fusion | flops 1879048192 | bytes 17039360 | tf_op jit(solution)/shard_map/dot_general | solution.py:34
  85.2 11.3 %fusion.5 = f32[128,3584]{1,0:T(8,128)} fusion(bf16[128,2048]{1,0:T(8,128)(2,1)S(1)} %all_gather.6, bf16[3584,2048]{1,0:T(8,128)(2,1)} %param.9), kind=kOutput, calls=%fused_computation.12 | convolution fusion | flops 1879048192 | bytes 17039360 | tf_op jit(solution)/shard_map/dot_general | solution.py:17
  96.6 0.0 all-reduce.3.cloned.1.call-update
  96.6 0.2 reduce-scatter.2.cloned.1.call-start
  96.8 108.4 %all-reduce.3.cloned.1.call-done = (f32[128,3584]{1,0:T(8,128)}, f32[128,3584]{1,0:T(8,128)}, f32[128,3584]{1,0:T(8,128)}) async-done(((f32[128,3584]{1,0:T(8,128)}, f32[128,3584]{1,0:T(8,128)}, f32[128,3584]{1,0:T(8,128)}), (f32[128,3584]{1,0:T(8,128)}, f32[128,3584]{1,0:T(8,128)}, f32[128,3584]{1,0:T(8,128)})) %all-reduce.3.cloned.1.call-update) | async-done | bytes 5505040 | tf_op jit(solution)/shard_map/psum | solution.py:36
  205.2 3.6 %multiply_convert_fusion.1 = (bf16[128,3584]{1,0:T(8,128)(2,1)S(1)}, bf16[128,3584]{1,0:T(8,128)(2,1)S(1)}) fusion(f32[128,3584]{1,0:T(8,128)} %get-tuple-element.9, f32[128,3584]{1,0:T(8,128)} %get-tuple-element.8, f32[128,3584]{1,0:T(8,128)} %get-tuple-element.10), kind=kLoop, calls=%fused_computation.7 | loop fusion | flops 5963776 | bytes 7340032 | tf_op jit(solution)/shard_map/convert_element_type | solution.py:12
  208.8 9.9 %fusion.8 = f32[128,2048]{1,0:T(8,128)S(1)} fusion(bf16[128,3584]{1,0:T(8,128)(2,1)S(1)} %get-tuple-element.12, bf16[2048,3584]{1,0:T(8,128)(2,1)} %param.7), kind=kOutput, calls=%fused_computation.15 | convolution fusion | flops 1879048192 | bytes 16646144 | tf_op jit(solution)/shard_map/dot_general | solution.py:17
  218.7 7.6 %fusion = bf16[2048,3584]{0,1:T(8,128)(2,1)} fusion(bf16[128,3584]{1,0:T(8,128)(2,1)S(1)} %get-tuple-element.12, bf16[128,2048]{1,0:T(8,128)(2,1)S(1)} %all_gather.7), kind=kOutput, calls=%fused_computation.3 | convolution fusion | flops 1886388224 | bytes 16121856 | tf_op jit(solution)/shard_map/dot_general | solution.py:23
  226.3 10.9 %convolution_add_fusion = f32[128,2048]{1,0:T(8,128)} fusion(f32[128,2048]{1,0:T(8,128)S(1)} %fusion.8, bf16[128,3584]{1,0:T(8,128)(2,1)S(1)} %get-tuple-element.11, bf16[2048,3584]{1,0:T(8,128)(2,1)} %param.8), kind=kOutput, calls=%fused_computation.5 | convolution fusion | flops 1879310336 | bytes 17694720 | tf_op jit(solution)/shard_map/dot_general | solution.py:17
  237.2 0.0 reduce-scatter.2.cloned.1.call-update
  237.2 18.7 %copy.9 = bf16[2048,3584]{1,0:T(8,128)(2,1)} copy(bf16[2048,3584]{0,1:T(8,128)(2,1)} %fusion) | data formatting | bytes 29360128
  255.9 7.6 %fusion.1 = bf16[2048,3584]{0,1:T(8,128)(2,1)} fusion(bf16[128,3584]{1,0:T(8,128)(2,1)S(1)} %get-tuple-element.11, bf16[128,2048]{1,0:T(8,128)(2,1)S(1)} %all_gather.7), kind=kOutput, calls=%fused_computation.4 | convolution fusion | flops 1886388224 | bytes 16121856 | tf_op jit(solution)/shard_map/dot_general | solution.py:23
  263.4 0.0 copy-start.1
  263.4 18.8 %copy.10 = bf16[2048,3584]{1,0:T(8,128)(2,1)} copy(bf16[2048,3584]{0,1:T(8,128)(2,1)} %fusion.1) | data formatting | bytes 29360128
  282.3 0.0 copy-done.1
  282.3 9.1 %convolution_convert_fusion = bf16[3584,2048]{1,0:T(8,128)(2,1)} fusion(bf16[128,2048]{1,0:T(8,128)(2,1)S(1)} %all_gather.6, f32[128,3584]{1,0:T(8,128)} %get-tuple-element.10, f32[128,3584]{1,0:T(8,128)S(1)} %copy-done.1), kind=kOutput, calls=%fused_computation | convolution fusion | flops 1889140736 | bytes 18874368 | tf_op jit(solution)/shard_map/dot_general | solution.py:23
  291.3 9.7 %reduce-scatter.2.cloned.1.call-done = f32[16,2048]{1,0:T(8,128)} async-done(((f32[128,2048]{1,0:T(8,128)}), f32[16,2048]{1,0:T(8,128)}) %reduce-scatter.2.cloned.1.call-update) | async-done | bytes 131088 | tf_op jit(solution)/shard_map/reduce_scatter | solution.py:41
  301.0 1.5 convert_element_type.29
Async XLA Ops:
  7.2 198.0 %all-reduce.3.cloned.1.call-start = ((), (), s32[]{:S(2)}) async-start(), calls=%async_computation.2 | async-start | bytes 11010048 | tf_op jit(solution)/shard_map/psum | solution.py:36
  71.8 10.0 %copy-start = (bf16[2048,3584]{1,0:T(8,128)(2,1)S(1)}, bf16[2048,3584]{1,0:T(8,128)(2,1)}, u32[]{:S(2)}) copy-start(bf16[2048,3584]{1,0:T(8,128)(2,1)} %param.8) | copy-start | bytes 44040196
  96.6 204.4 %reduce-scatter.2.cloned.1.call-start = ((), (), s32[]{:S(2)}) async-start(), calls=%async_computation.1 | async-start | bytes 1179648 | tf_op jit(solution)/shard_map/reduce_scatter | solution.py:41
  263.4 18.8 %copy-start.1 = (f32[128,3584]{1,0:T(8,128)S(1)}, f32[128,3584]{1,0:T(8,128)}, u32[]{:S(2)}) copy-start(f32[128,3584]{1,0:T(8,128)} %get-tuple-element.8) | copy-start | bytes 5505028
Sparse Core Ops, SparseCore 0:
  96.7 108.4 all-reduce.2
  237.3 63.6 reduce-scatter.1
where the time goes:
time: 311 us; the launch traced here: 309 us
  waiting for transfers between devices  118 us (38%)
  matrix products  68.4 us (22%)
  blocking collectives  64.6 us (21%)
  local copies, waits for them, and re-layouts  38.9 us (13%)
  between operations  14.1 us (5%)
  other arithmetic  5.1 us (2%)
    psum x1, waiting for transfers between devices, local(): gate, up, hidden_grad = lax.psum((gate_part, up_part, hidden_part), 'row')  108 us
    unnamed x6, local copies, waits for them, and re-layouts  38.9 us
    all_gather x1, blocking collectives, local(): lax.all_gather(tokens, 'col', axis=0, tiled=True)  33.2 us
    dot_general x3, matrix products, contract_last(): lax.dot_general(left, right, (((1,), (1,)), ((), ())), preferred_element_...  32.1 us
    all_gather x1, blocking collectives, local(): lax.all_gather(out_grad, 'col', axis=0, tiled=True)  31.4 us
    dot_general x3, matrix products, contract_first(): lax.dot_general(left, right, (((0,), (0,)), ((), ())), preferred_element_...  24.2 us
    reduce_scatter x1, waiting for transfers between devices, local(): lax.psum_scatter(contract_last(d_gate, gate_weight) + contract_last(d_up,...  9.66 us
    dot_general x1, matrix products, local(): jnp.dot(full_tokens, gate_weight, preferred_element_type=jnp.float32)  8.63 us
  transfers between devices with their start and end apart: 2, of which 2 were waited for; matrix products, arithmetic and copies ran while one was open for 17% of the time, Pallas kernels for 0%

commit v1 on v0

v1 whole, which is shorter than its diff:
```python
import functools

import jax
import jax.numpy as jnp
from jax import lax
from jax.experimental import pallas as pl
from jax.experimental.pallas import tpu as pltpu
from jax.sharding import PartitionSpec as P

MESH = pl.DeviceIdType.MESH
F32, BF16 = jnp.float32, jnp.bfloat16


def pointwise(gate, up, hidden_grad):
    logistic = jax.nn.sigmoid(gate)
    active = gate * logistic
    hidden = (active * up).astype(BF16)
    d_gate = (hidden_grad * up * logistic * (1.0 + gate * (1.0 - logistic))).astype(BF16)
    d_up = (hidden_grad * active).astype(BF16)
    return hidden, d_gate, d_up


def contract_last(left, right):
    return lax.dot_general(left, right, (((1,), (1,)), ((), ())), preferred_element_type=F32)


def chunk_width(units):
    for width in (512, 256, 128):
        if units % width == 0:
            return width
    return units


def loop(low, high, body):
    def step(index, carry):
        body(index)
        return carry

    lax.fori_loop(low, high, step, 0)


def forward_kernel(
    n, group, chunks, width,
    tokens, out_grad, gate_w, up_w, down_w,
    tok_out, grad_out, hid_out, dgate_out, dup_out, *rest,
):
    partial_outs = rest[:n]
    (
        tok, grad, wg, wu, wd, part, core_in, x_send, x_in, res, acc,
        w_sem, own_sem, ag_send, ag_fwd, ag_recv,
        core_send_sem, core_recv_sem, x_send_sem, x_recv_sem, res_send_sem, res_recv_sem,
        out_sem, full_sem,
    ) = rest[n:]
    block = tokens.shape[0]
    total = block * n
    half = total // 2
    row, me = lax.axis_index("row"), lax.axis_index("col")
    core = lax.rem(row, 2)
    core_peer = row + 1 - 2 * core
    x_peer = lax.rem(row + 2, 4)
    groups = n // group
    hi, lo = me // group, lax.rem(me, group)
    mine = pl.ds(pl.multiple_of(core * half, half), half)
    theirs = pl.ds(pl.multiple_of((1 - core) * half, half), half)

    def columns(c):
        return pl.ds(pl.multiple_of(c * width, width), width)

    def weight_copy(m, c):
        if m == 2:
            return pltpu.make_async_copy(
                down_w.at[columns(c), :], wd.at[columns(c), :], w_sem.at[m, c]
            )
        source, target = ((gate_w, wg), (up_w, wu))[m]
        return pltpu.make_async_copy(
            source.at[:, columns(c)], target.at[:, columns(c)], w_sem.at[m, c]
        )

    def load_pair(c):
        weight_copy(0, c).start()
        weight_copy(1, c).start()

    def place(owner):
        return pl.ds(pl.multiple_of(owner * block, block), block)

    def far(k):
        return lax.rem(hi + k, groups) * group + lo

    def far_from(k):
        return lax.rem(hi + groups - k, groups) * group + lo

    def near(j):
        return hi * group + lax.rem(lo + j, group)

    arrays = ((tokens, tok), (out_grad, grad))

    def own_copy(a):
        return pltpu.make_async_copy(arrays[a][0], arrays[a][1].at[place(me), :], own_sem.at[a])

    def own_send(a, peer):
        return pltpu.make_async_remote_copy(
            src_ref=arrays[a][0],
            dst_ref=arrays[a][1].at[place(me), :],
            send_sem=ag_send.at[a, peer],
            recv_sem=ag_recv.at[a, me],
            device_id={"col": peer},
            device_id_type=MESH,
        )

    def forward_send(a, owner, j):
        return pltpu.make_async_remote_copy(
            src_ref=arrays[a][1].at[place(owner), :],
            dst_ref=arrays[a][1].at[place(owner), :],
            send_sem=ag_fwd.at[a, owner, j],
            recv_sem=ag_recv.at[a, owner],
            device_id={"col": near(j)},
            device_id_type=MESH,
        )

    def wait_block(a, owner):
        pltpu.make_async_copy(
            arrays[a][0], arrays[a][1].at[place(owner), :], ag_recv.at[a, owner]
        ).wait()

    def gather_start(a):
        own_copy(a).start()
        loop(1, groups, lambda k: own_send(a, far(k)).start())
        loop(1, group, lambda j: own_send(a, near(j)).start())

    def gather_forward(a):
        def one(k):
            owner = far_from(k)
            wait_block(a, owner)
            loop(1, group, lambda j: forward_send(a, owner, j).start())

        loop(1, groups, one)

    def gather_finish(a):
        def one(j):
            peer = near(j)
            wait_block(a, peer)
            loop(1, groups, lambda k: wait_block(
                a, lax.rem(hi + groups - k, groups) * group + lax.rem(lo + j, group)))

        loop(1, group, one)
        own_copy(a).wait()

    def gather_drain(a):
        loop(1, groups, lambda k: own_send(a, far(k)).wait_send())
        loop(1, group, lambda j: own_send(a, near(j)).wait_send())
        loop(1, groups, lambda k: loop(
            1, group, lambda j: forward_send(a, far_from(k), j).wait_send()))

    def core_copy(m, c):
        return pltpu.make_async_remote_copy(
            src_ref=part.at[m, c, theirs, :],
            dst_ref=core_in.at[m, c],
            send_sem=core_send_sem.at[m, c],
            recv_sem=core_recv_sem.at[m, c],
            device_id={"row": core_peer},
            device_id_type=MESH,
        )

    def x_copy(m, c):
        return pltpu.make_async_remote_copy(
            src_ref=x_send.at[m, c],
            dst_ref=x_in.at[m, c],
            send_sem=x_send_sem.at[m, c],
            recv_sem=x_recv_sem.at[m, c],
            device_id={"row": x_peer},
            device_id_type=MESH,
        )

    def res_copy(c):
        return pltpu.make_async_remote_copy(
            src_ref=res.at[c, :, mine, :],
            dst_ref=res.at[c, :, mine, :],
            send_sem=res_send_sem.at[c],
            recv_sem=res_recv_sem.at[c],
            device_id={"row": core_peer},
            device_id_type=MESH,
        )

    def out_copy(k, c):
        target = (hid_out, dgate_out, dup_out)[k]
        return pltpu.make_async_copy(res.at[c, k], target.at[:, columns(c)], out_sem.at[k, c])

    def multiply(m, c):
        weight_copy(m, c).wait()
        if m == 2:
            part[m, c] = contract_last(grad[...], wd[columns(c), :])
        else:
            weight = (wg, wu)[m]
            part[m, c] = jnp.dot(tok[...], weight[:, columns(c)], preferred_element_type=F32)
        core_copy(m, c).start()

    def chip_sum(m, c):
        core_copy(m, c).wait_recv()
        value = part[m, c, mine, :] + core_in[m, c]
        part[m, c, mine, :] = value
        x_send[m, c] = value.astype(BF16)
        x_copy(m, c).start()

    def gate_up(c):
        multiply(0, c)
        multiply(1, c)

        @pl.when(c > 0)
        def _():
            chip_sum(0, c - 1)
            chip_sum(1, c - 1)

    def down(c):
        multiply(2, c)

        @pl.when(c == 0)
        def _():
            chip_sum(0, chunks - 1)
            chip_sum(1, chunks - 1)

        @pl.when(c > 0)
        def _():
            chip_sum(2, c - 1)

    def input_product(c):
        res_copy(c).wait_recv()
        for k in range(3):
            out_copy(k, c).start()
        acc[...] += contract_last(res[c, 1], wg[:, columns(c)])
        acc[...] += contract_last(res[c, 2], wu[:, columns(c)])

    def finish(c):
        for m in range(3):
            x_copy(m, c).wait_recv()
        values = [part[m, c, mine, :] + x_in[m, c].astype(F32) for m in range(3)]
        for k, value in enumerate(pointwise(*values)):
            res[c, k, mine, :] = value
        res_copy(c).start()

        @pl.when(c > 0)
        def _():
            input_product(c - 1)

    loop(0, chunks, load_pair)
    loop(0, chunks, lambda c: weight_copy(2, c).start())
    acc[...] = jnp.zeros_like(acc)

    barrier = pltpu.get_barrier_semaphore()
    loop(1, groups, lambda k: pl.semaphore_signal(
        barrier, inc=1, device_id={"col": far(k)}, device_id_type=MESH))
    loop(1, group, lambda j: pl.semaphore_signal(
        barrier, inc=1, device_id={"col": near(j)}, device_id_type=MESH))
    for peer in (core_peer, x_peer):
        pl.semaphore_signal(barrier, inc=1, device_id={"row": peer}, device_id_type=MESH)
    pl.semaphore_wait(barrier, groups + group)

    gather_start(0)
    gather_forward(0)
    gather_start(1)
    gather_finish(0)
    early = min(3, chunks)
    loop(0, early, gate_up)
    gather_forward(1)
    loop(early, chunks, gate_up)
    gather_finish(1)
    tok_copy = pltpu.make_async_copy(tok, tok_out, full_sem.at[0])
    grad_copy = pltpu.make_async_copy(grad, grad_out, full_sem.at[1])
    tok_copy.start()
    grad_copy.start()
    loop(0, chunks, down)
    chip_sum(2, chunks - 1)
    loop(0, chunks, finish)
    input_product(chunks - 1)

    for k in range(n):
        owner = lax.rem(me + k, n)
        partial_outs[k][...] = acc[place(owner), :].astype(BF16)

    gather_drain(0)
    gather_drain(1)

    def drain(c):
        for m in range(3):
            core_copy(m, c).wait_send()
            x_copy(m, c).wait_send()
            out_copy(m, c).wait()
        res_copy(c).wait_send()

    loop(0, chunks, drain)
    tok_copy.wait()
    grad_copy.wait()


def forward(n, tokens, out_grad, gate_w, up_w, down_w):
    block, depth = tokens.shape
    units = gate_w.shape[1]
    total = block * n
    width = chunk_width(units)
    chunks = units // width
    group = 2 if n % 2 == 0 else 1
    half = total // 2
    anywhere = pl.BlockSpec(memory_space=pl.ANY)
    inside = pl.BlockSpec(memory_space=pltpu.VMEM)
    full = jax.ShapeDtypeStruct((total, depth), BF16)
    hidden = jax.ShapeDtypeStruct((total, units), BF16)
    piece = jax.ShapeDtypeStruct((block, depth), BF16)
    dma = pltpu.SemaphoreType.DMA
    return pl.pallas_call(
        functools.partial(forward_kernel, n, group, chunks, width),
        out_shape=[full] * 2 + [hidden] * 3 + [piece] * n,
        in_specs=[anywhere] * 5,
        out_specs=[anywhere] * 5 + [inside] * n,
        scratch_shapes=[
            pltpu.VMEM((total, depth), BF16),
            pltpu.VMEM((total, depth), BF16),
            pltpu.VMEM((depth, units), BF16),
            pltpu.VMEM((depth, units), BF16),
            pltpu.VMEM((units, depth), BF16),
            pltpu.VMEM((3, chunks, total, width), F32),
            pltpu.VMEM((3, chunks, half, width), F32),
            pltpu.VMEM((3, chunks, half, width), BF16),
            pltpu.VMEM((3, chunks, half, width), BF16),
            pltpu.VMEM((chunks, 3, total, width), BF16),
            pltpu.VMEM((total, depth), F32),
            dma((3, chunks)),
            dma((2,)),
            dma((2, n)),
            dma((2, n, group)),
            dma((2, n)),
            dma((3, chunks)),
            dma((3, chunks)),
            dma((3, chunks)),
            dma((3, chunks)),
            dma((chunks,)),
            dma((chunks,)),
            dma((3, chunks)),
            dma((2,)),
        ],
        compiler_params=pltpu.CompilerParams(
            collective_id=0, has_side_effects=True, vmem_limit_bytes=63 * 2**20
        ),
        name="forward_exchange",
    )(tokens, out_grad, gate_w, up_w, down_w)


def grads_kernel(tok, grad, hidden, d_gate, d_up, gate_o, up_o, down_o, tok_t, hid_t):
    step = pl.program_id(0)

    @pl.when(step == 0)
    def _():
        tok_t[...] = tok[...].T
        hid_t[...] = hidden[...].T

    rows = gate_o.shape[0]
    left = tok_t[pl.ds(pl.multiple_of(step * rows, rows), rows), :]
    gate_o[...] = jnp.dot(left, d_gate[...], preferred_element_type=F32).astype(BF16)
    up_o[...] = jnp.dot(left, d_up[...], preferred_element_type=F32).astype(BF16)
    units = down_o.shape[0]
    left = hid_t[pl.ds(pl.multiple_of(step * units, units), units), :]
    down_o[...] = jnp.dot(left, grad[...], preferred_element_type=F32).astype(BF16)


def weight_grads(tok, grad, hidden, d_gate, d_up):
    total, depth = tok.shape
    units = hidden.shape[1]
    steps = max(s for s in (1, 2, 4, 8) if depth % (16 * s) == 0 and units % (16 * s) == 0)
    inside = pl.BlockSpec(memory_space=pltpu.VMEM)
    wide = pl.BlockSpec((depth // steps, units), lambda i: (i, 0))
    tall = pl.BlockSpec((units // steps, depth), lambda i: (i, 0))
    return pl.pallas_call(
        grads_kernel,
        grid=(steps,),
        out_shape=[
            jax.ShapeDtypeStruct((depth, units), BF16),
            jax.ShapeDtypeStruct((depth, units), BF16),
            jax.ShapeDtypeStruct((units, depth), BF16),
        ],
        in_specs=[inside] * 5,
        out_specs=[wide, wide, tall],
        scratch_shapes=[pltpu.VMEM((depth, total), BF16), pltpu.VMEM((units, total), BF16)],
        compiler_params=pltpu.CompilerParams(vmem_limit_bytes=48 * 2**20),
        cost_estimate=pl.CostEstimate(
            flops=6 * total * depth * units, bytes_accessed=6 * depth * units, transcendentals=0
        ),
        name="weight_grads",
    )(tok, grad, hidden, d_gate, d_up)


def local(n, tokens, out_grad, gate_weight, up_weight, down_weight):
    tok, grad, hidden, d_gate, d_up, *pieces = forward(
        n, tokens, out_grad, gate_weight, up_weight, down_weight
    )
    arrived = [
        lax.ppermute(pieces[k], "col", [(i, (i + k) % n) for i in range(n)]) for k in range(1, n)
    ]
    grad_gate, grad_up, grad_down = weight_grads(tok, grad, hidden, d_gate, d_up)
    total = pieces[0].astype(F32)
    for piece in arrived:
        total = total + piece.astype(F32)
    return total.astype(BF16), grad_gate, grad_up, grad_down


def solution(mesh):
    in_specs = (P("col", "row"), P("col", "row"), P("row", "col"), P("row", "col"), P("col", "row"))
    out_specs = (P("col", "row"), P("row", "col"), P("row", "col"), P("col", "row"))
    return jax.shard_map(
        functools.partial(local, mesh.shape["col"]),
        mesh=mesh, in_specs=in_specs, out_specs=out_specs, check_vma=False,
    )
```

time: 311 us -> 93.5 us (0.30)
  waiting for transfers between devices: 118 us -> 0.02 us
  Pallas kernels: 0 us -> 74.9 us
  matrix products: 68.4 us -> 0 us
  blocking collectives: 64.6 us -> 0 us
  local copies, waits for them, and re-layouts: 38.9 us -> 5.62 us
  between operations: 14.1 us -> 0.68 us
  starting transfers between devices: 0.26 us -> 11.3 us
  other arithmetic: 5.1 us -> 0.7 us
    psum x1 -> x0, waiting for transfers between devices: 108 us -> none  [local(): gate, up, hidden_grad = lax.psum((gate_part, up_part, hidden_part), 'row')]
    pallas_call x0 -> x2, Pallas kernels: none -> 74.9 us  [the longest x1 57.6 us: forward(): pl.pallas_call(functools.partial(forward_kernel, n, group, chunks, width)...]
    dot_general x8 -> x0, matrix products: 68.4 us -> none  [the longest x3 32.1 us: contract_last(): lax.dot_general(left, right, (((1,), (1,)), ((), ())), preferred_element_...]
    all_gather x2 -> x0, blocking collectives: 64.6 us -> none  [the longest x1 33.2 us: local(): lax.all_gather(tokens, 'col', axis=0, tiled=True)]
    unnamed x6 -> x12, local copies, waits for them, and re-layouts: 38.9 us -> 5.62 us
    ppermute x0 -> x7, starting transfers between devices: none -> 11.3 us  [local(): lax.ppermute(pieces[k], 'col', [(i, (i + k) % n) for i in range(n)])]
    reduce_scatter x1 -> x0, waiting for transfers between devices: 9.66 us -> none  [local(): lax.psum_scatter(contract_last(d_gate, gate_weight) + contract_last(d_up,...]
    convert_element_type x2 -> x1, other arithmetic: 5.1 us -> 0.7 us  [local(): return (total.astype(BF16), grad_gate, grad_up, grad_down)]
  transfers between devices with their start and end apart: 2 -> 7, of which waited for: 2 -> 0; matrix products, arithmetic and copies ran while one was open for 17% -> 0% of each run, Pallas kernels for 0% -> 19%
where the time goes in v1:
time: 93.5 us; the launch traced here: 93.2 us
  Pallas kernels  74.9 us (80%)
  starting transfers between devices  11.3 us (12%)
  local copies, waits for them, and re-layouts  5.62 us (6%)
    pallas_call x1, Pallas kernels, forward(): pl.pallas_call(functools.partial(forward_kernel, n, group, chunks, width)...  57.6 us
    pallas_call x1, Pallas kernels, weight_grads(): pl.pallas_call(grads_kernel, grid=(steps,), out_shape=[jax.ShapeDtypeStru...  17.3 us
    ppermute x7, starting transfers between devices, local(): lax.ppermute(pieces[k], 'col', [(i, (i + k) % n) for i in range(n)])  11.3 us
    unnamed x12, local copies, waits for them, and re-layouts  5.62 us
  transfers between devices with their start and end apart: 7, of which 0 were waited for; matrix products, arithmetic and copies ran while one was open for 0% of the time, Pallas kernels for 19%

profile of v1, /device:TPU:0, one launch (start us, length us, event | category | flops | bytes accessed | tf_op | source)
XLA Modules:
  0.0 93.2 jit_solution(17850163298688725226)
XLA Ops:
  0.6 57.6 %forward_exchange.1 = (bf16[128,2048]{1,0:T(8,128)(2,1)}, bf16[128,2048]{1,0:T(8,128)(2,1)}, bf16[128,3584]{1,0:T(8,128)(2,1)}, bf16[128,3584]{1,0:T(8,128)(2,1)...) custom-call(bf16[16,2048]{1,0:T(8,128)(2,1)} %tokens.1, ...), custom_call_target="tpu_custom_call" | custom-call | tf_op jit(solution)/shard_map/forward_exchange/pallas_call | solution.py:308
  58.2 0.6 collective-permute-start
  58.8 1.5 %collective-permute-start.1 = (bf16[16,2048]{1,0:T(8,128)(2,1)}, bf16[16,2048]{1,0:T(8,128)(2,1)S(1)}, u32[]{:S(2)}, u32[]{:S(2)}) collective-permute-start(bf16[16,2048]{1,0:T(8,128)(2,1)} %get-tuple-element.22), channel_id=1, source_target_pairs={{0,2},{1,3},{2,4},{3,5},{4,6},{5,7},{6,0},{7,1},{8,10},{9,11},{10,... | collective-permute-start | bytes 196616 | tf_op jit(solution)/shard_map/ppermute | solution.py:394
  60.3 2.6 %collective-permute-start.2 = (bf16[16,2048]{1,0:T(8,128)(2,1)}, bf16[16,2048]{1,0:T(8,128)(2,1)S(1)}, u32[]{:S(2)}, u32[]{:S(2)}) collective-permute-start(bf16[16,2048]{1,0:T(8,128)(2,1)} %get-tuple-element.23), channel_id=1, source_target_pairs={{0,3},{1,4},{2,5},{3,6},{4,7},{5,0},{6,1},{7,2},{8,11},{9,12},{10,... | collective-permute-start | bytes 196616 | tf_op jit(solution)/shard_map/ppermute | solution.py:394
  62.9 1.3 %collective-permute-start.3 = (bf16[16,2048]{1,0:T(8,128)(2,1)}, bf16[16,2048]{1,0:T(8,128)(2,1)S(1)}, u32[]{:S(2)}, u32[]{:S(2)}) collective-permute-start(bf16[16,2048]{1,0:T(8,128)(2,1)} %get-tuple-element.24), channel_id=1, source_target_pairs={{0,4},{1,5},{2,6},{3,7},{4,0},{5,1},{6,2},{7,3},{8,12},{9,13},{10,... | collective-permute-start | bytes 196616 | tf_op jit(solution)/shard_map/ppermute | solution.py:394
  64.2 2.5 %collective-permute-start.4 = (bf16[16,2048]{1,0:T(8,128)(2,1)}, bf16[16,2048]{1,0:T(8,128)(2,1)S(1)}, u32[]{:S(2)}, u32[]{:S(2)}) collective-permute-start(bf16[16,2048]{1,0:T(8,128)(2,1)} %get-tuple-element.25), channel_id=1, source_target_pairs={{0,5},{1,6},{2,7},{3,0},{4,1},{5,2},{6,3},{7,4},{8,13},{9,14},{10,... | collective-permute-start | bytes 196616 | tf_op jit(solution)/shard_map/ppermute | solution.py:394
  66.7 0.0 collective-permute-done
  66.7 1.4 %collective-permute-start.5 = (bf16[16,2048]{1,0:T(8,128)(2,1)}, bf16[16,2048]{1,0:T(8,128)(2,1)S(1)}, u32[]{:S(2)}, u32[]{:S(2)}) collective-permute-start(bf16[16,2048]{1,0:T(8,128)(2,1)} %get-tuple-element.26), channel_id=1, source_target_pairs={{0,6},{1,7},{2,0},{3,1},{4,2},{5,3},{6,4},{7,5},{8,14},{9,15},{10,... | collective-permute-start | bytes 196616 | tf_op jit(solution)/shard_map/ppermute | solution.py:394
  68.1 0.0 collective-permute-done.1
  68.1 1.4 %collective-permute-start.6 = (bf16[16,2048]{1,0:T(8,128)(2,1)}, bf16[16,2048]{1,0:T(8,128)(2,1)S(1)}, u32[]{:S(2)}, u32[]{:S(2)}) collective-permute-start(bf16[16,2048]{1,0:T(8,128)(2,1)} %get-tuple-element.27), channel_id=1, source_target_pairs={{0,7},{1,0},{2,1},{3,2},{4,3},{5,4},{6,5},{7,6},{8,15},{9,8},{10,9... | collective-permute-start | bytes 196616 | tf_op jit(solution)/shard_map/ppermute | solution.py:394
  69.5 0.0 copy-start
  69.5 1.2 %copy-done = bf16[128,3584]{1,0:T(8,128)(2,1)S(1)} copy-done((bf16[128,3584]{1,0:T(8,128)(2,1)S(1)}, bf16[128,3584]{1,0:T(8,128)(2,1)}, u32[]{:S(2)}) %copy-start) | copy-done | bytes 917528
  70.7 1.2 %copy-done.1 = bf16[128,3584]{1,0:T(8,128)(2,1)S(1)} copy-done((bf16[128,3584]{1,0:T(8,128)(2,1)S(1)}, bf16[128,3584]{1,0:T(8,128)(2,1)}, u32[]{:S(2)}) %copy-start.1) | copy-done | bytes 917528
  71.9 1.2 %copy-done.2 = bf16[128,3584]{1,0:T(8,128)(2,1)S(1)} copy-done((bf16[128,3584]{1,0:T(8,128)(2,1)S(1)}, bf16[128,3584]{1,0:T(8,128)(2,1)}, u32[]{:S(2)}) %copy-start.2) | copy-done | bytes 917528
  73.0 1.0 %copy-done.3 = bf16[128,2048]{1,0:T(8,128)(2,1)S(1)} copy-done((bf16[128,2048]{1,0:T(8,128)(2,1)S(1)}, bf16[128,2048]{1,0:T(8,128)(2,1)}, u32[]{:S(2)}) %copy-start.3) | copy-done | bytes 524312
  74.1 1.0 %copy-done.4 = bf16[128,2048]{1,0:T(8,128)(2,1)S(1)} copy-done((bf16[128,2048]{1,0:T(8,128)(2,1)S(1)}, bf16[128,2048]{1,0:T(8,128)(2,1)}, u32[]{:S(2)}) %copy-start.4) | copy-done | bytes 524312
  75.1 17.3 %weight_grads.1 = (bf16[2048,3584]{1,0:T(8,128)(2,1)}, bf16[2048,3584]{1,0:T(8,128)(2,1)}, bf16[3584,2048]{1,0:T(8,128)(2,1)}) custom-call(bf16[128,2048]{1,0:T(8,128)(2,1)S(1)} %copy-done.3, bf16[128,2048]{1,0:T(8,128)(2,1)S(1)} %copy-done.4, bf16[128,3584]{1,0:T(8,128)(2,1)S(1)} %copy-done, bf16[128,3584]{1,0:T(8,128)(2,1)S(1)} %copy-done.1, ...), custom_call_target="tpu_custom_call" | custom-call | flops 5637144576 | bytes 44040192 | tf_op jit(solution)/shard_map/weight_grads/pallas_call | solution.py:370
  92.5 0.0 collective-permute-done.2
  92.5 0.0 collective-permute-done.3
  92.5 0.0 collective-permute-done.4
  92.5 0.0 collective-permute-done.5
  92.5 0.0 collective-permute-done.6
  92.5 0.0 copy-done.5
  92.5 0.7 add_convert_fusion
  (5 shorter events, 0.0 us)
Async XLA Ops:
  58.2 8.5 %collective-permute-start = (bf16[16,2048]{1,0:T(8,128)(2,1)}, bf16[16,2048]{1,0:T(8,128)(2,1)S(1)}, u32[]{:S(2)}, u32[]{:S(2)}) collective-permute-start(bf16[16,2048]{1,0:T(8,128)(2,1)} %get-tuple-element.21), channel_id=1, source_target_pairs={{0,1},{1,2},{2,3},{3,4},{4,5},{5,6},{6,7},{7,0},{8,9},{9,10},{10,1... | collective-permute-start | bytes 196616 | tf_op jit(solution)/shard_map/ppermute | solution.py:394
  58.8 9.3 %collective-permute-start.1 = (bf16[16,2048]{1,0:T(8,128)(2,1)}, bf16[16,2048]{1,0:T(8,128)(2,1)S(1)}, u32[]{:S(2)}, u32[]{:S(2)}) collective-permute-start(bf16[16,2048]{1,0:T(8,128)(2,1)} %get-tuple-element.22), channel_id=1, source_target_pairs={{0,2},{1,3},{2,4},{3,5},{4,6},{5,7},{6,0},{7,1},{8,10},{9,11},{10,... | collective-permute-start | bytes 196616 | tf_op jit(solution)/shard_map/ppermute | solution.py:394
  60.3 32.2 %collective-permute-start.2 = (bf16[16,2048]{1,0:T(8,128)(2,1)}, bf16[16,2048]{1,0:T(8,128)(2,1)S(1)}, u32[]{:S(2)}, u32[]{:S(2)}) collective-permute-start(bf16[16,2048]{1,0:T(8,128)(2,1)} %get-tuple-element.23), channel_id=1, source_target_pairs={{0,3},{1,4},{2,5},{3,6},{4,7},{5,0},{6,1},{7,2},{8,11},{9,12},{10,... | collective-permute-start | bytes 196616 | tf_op jit(solution)/shard_map/ppermute | solution.py:394
  62.9 29.6 %collective-permute-start.3 = (bf16[16,2048]{1,0:T(8,128)(2,1)}, bf16[16,2048]{1,0:T(8,128)(2,1)S(1)}, u32[]{:S(2)}, u32[]{:S(2)}) collective-permute-start(bf16[16,2048]{1,0:T(8,128)(2,1)} %get-tuple-element.24), channel_id=1, source_target_pairs={{0,4},{1,5},{2,6},{3,7},{4,0},{5,1},{6,2},{7,3},{8,12},{9,13},{10,... | collective-permute-start | bytes 196616 | tf_op jit(solution)/shard_map/ppermute | solution.py:394
  64.2 28.2 %collective-permute-start.4 = (bf16[16,2048]{1,0:T(8,128)(2,1)}, bf16[16,2048]{1,0:T(8,128)(2,1)S(1)}, u32[]{:S(2)}, u32[]{:S(2)}) collective-permute-start(bf16[16,2048]{1,0:T(8,128)(2,1)} %get-tuple-element.25), channel_id=1, source_target_pairs={{0,5},{1,6},{2,7},{3,0},{4,1},{5,2},{6,3},{7,4},{8,13},{9,14},{10,... | collective-permute-start | bytes 196616 | tf_op jit(solution)/shard_map/ppermute | solution.py:394
  66.7 25.8 %collective-permute-start.5 = (bf16[16,2048]{1,0:T(8,128)(2,1)}, bf16[16,2048]{1,0:T(8,128)(2,1)S(1)}, u32[]{:S(2)}, u32[]{:S(2)}) collective-permute-start(bf16[16,2048]{1,0:T(8,128)(2,1)} %get-tuple-element.26), channel_id=1, source_target_pairs={{0,6},{1,7},{2,0},{3,1},{4,2},{5,3},{6,4},{7,5},{8,14},{9,15},{10,... | collective-permute-start | bytes 196616 | tf_op jit(solution)/shard_map/ppermute | solution.py:394
  68.1 24.4 %collective-permute-start.6 = (bf16[16,2048]{1,0:T(8,128)(2,1)}, bf16[16,2048]{1,0:T(8,128)(2,1)S(1)}, u32[]{:S(2)}, u32[]{:S(2)}) collective-permute-start(bf16[16,2048]{1,0:T(8,128)(2,1)} %get-tuple-element.27), channel_id=1, source_target_pairs={{0,7},{1,0},{2,1},{3,2},{4,3},{5,4},{6,5},{7,6},{8,15},{9,8},{10,9... | collective-permute-start | bytes 196616 | tf_op jit(solution)/shard_map/ppermute | solution.py:394
  69.5 1.2 %copy-start = (bf16[128,3584]{1,0:T(8,128)(2,1)S(1)}, bf16[128,3584]{1,0:T(8,128)(2,1)}, u32[]{:S(2)}) copy-start(bf16[128,3584]{1,0:T(8,128)(2,1)} %get-tuple-element.30.hidden) | copy-start | bytes 2752516
  70.7 1.2 %copy-start.1 = (bf16[128,3584]{1,0:T(8,128)(2,1)S(1)}, bf16[128,3584]{1,0:T(8,128)(2,1)}, u32[]{:S(2)}) copy-start(bf16[128,3584]{1,0:T(8,128)(2,1)} %get-tuple-element.31.d_gate) | copy-start | bytes 2752516
  71.9 1.2 %copy-start.2 = (bf16[128,3584]{1,0:T(8,128)(2,1)S(1)}, bf16[128,3584]{1,0:T(8,128)(2,1)}, u32[]{:S(2)}) copy-start(bf16[128,3584]{1,0:T(8,128)(2,1)} %get-tuple-element.32.d_up) | copy-start | bytes 2752516
  73.0 1.0 %copy-start.3 = (bf16[128,2048]{1,0:T(8,128)(2,1)S(1)}, bf16[128,2048]{1,0:T(8,128)(2,1)}, u32[]{:S(2)}) copy-start(bf16[128,2048]{1,0:T(8,128)(2,1)} %get-tuple-element.28.tok) | copy-start | bytes 1572868
  74.1 1.0 %copy-start.4 = (bf16[128,2048]{1,0:T(8,128)(2,1)S(1)}, bf16[128,2048]{1,0:T(8,128)(2,1)}, u32[]{:S(2)}) copy-start(bf16[128,2048]{1,0:T(8,128)(2,1)} %get-tuple-element.29.grad) | copy-start | bytes 1572868
  75.1 17.4 %copy-start.5 = (bf16[16,2048]{1,0:T(8,128)(2,1)S(1)}, bf16[16,2048]{1,0:T(8,128)(2,1)}, u32[]{:S(2)}) copy-start(bf16[16,2048]{1,0:T(8,128)(2,1)} %get-tuple-element.20) | copy-start | bytes 196612

commit v2 on v1

--- a/solution.py
+++ b/solution.py
@@ -20,10 +20,6 @@
     return hidden, d_gate, d_up
 
 
-def contract_last(left, right):
-    return lax.dot_general(left, right, (((1,), (1,)), ((), ())), preferred_element_type=F32)
-
-
 def chunk_width(units):
     for width in (512, 256, 128):
         if units % width == 0:
@@ -42,16 +38,17 @@
 def forward_kernel(
     n, group, chunks, width,
     tokens, out_grad, gate_w, up_w, down_w,
-    tok_out, grad_out, hid_out, dgate_out, dup_out, *rest,
+    tok_out, grad_out, hid_out, dgate_out, dup_out, keep_out, send_out,
+    *scratch,
 ):
-    partial_outs = rest[:n]
     (
-        tok, grad, wg, wu, wd, part, core_in, x_send, x_in, res, acc,
+        tok, grad, tok_t, grad_t, hid_t, wg, wu, wd, part, core_in, x_send, x_in, res, turned, acc_t, acc,
         w_sem, own_sem, ag_send, ag_fwd, ag_recv,
         core_send_sem, core_recv_sem, x_send_sem, x_recv_sem, res_send_sem, res_recv_sem,
         out_sem, full_sem,
-    ) = rest[n:]
+    ) = scratch
     block = tokens.shape[0]
+    bands = 512 if tokens.shape[1] % 512 == 0 else tokens.shape[1]
     total = block * n
     half = total // 2
     row, me = lax.axis_index("row"), lax.axis_index("col")
@@ -182,13 +179,19 @@
         )
 
     def out_copy(k, c):
-        target = (hid_out, dgate_out, dup_out)[k]
+        if k == 0:
+            return pltpu.make_async_copy(
+                hid_t.at[columns(c), :], hid_out.at[columns(c), :], out_sem.at[k, c]
+            )
+        target = (dgate_out, dup_out)[k - 1]
         return pltpu.make_async_copy(res.at[c, k], target.at[:, columns(c)], out_sem.at[k, c])
 
     def multiply(m, c):
         weight_copy(m, c).wait()
         if m == 2:
-            part[m, c] = contract_last(grad[...], wd[columns(c), :])
+            part[m, c] = jnp.dot(
+                wd[columns(c), :], grad_t[...], preferred_element_type=F32
+            ).T
         else:
             weight = (wg, wu)[m]
             part[m, c] = jnp.dot(tok[...], weight[:, columns(c)], preferred_element_type=F32)
@@ -224,10 +227,20 @@
 
     def input_product(c):
         res_copy(c).wait_recv()
-        for k in range(3):
-            out_copy(k, c).start()
-        acc[...] += contract_last(res[c, 1], wg[:, columns(c)])
-        acc[...] += contract_last(res[c, 2], wu[:, columns(c)])
+        out_copy(1, c).start()
+        out_copy(2, c).start()
+        hid_t[columns(c), :] = res[c, 0].T
+        out_copy(0, c).start()
+        turned[0] = res[c, 1].T
+        turned[1] = res[c, 2].T
+
+        def band(r):
+            rows = pl.ds(pl.multiple_of(r * bands, bands), bands)
+            acc_t[rows, :] += jnp.dot(
+                wg[rows, columns(c)], turned[0], preferred_element_type=F32
+            ) + jnp.dot(wu[rows, columns(c)], turned[1], preferred_element_type=F32)
+
+        loop(0, acc_t.shape[0] // bands, band)
 
     def finish(c):
         for m in range(3):
@@ -243,7 +256,7 @@
 
     loop(0, chunks, load_pair)
     loop(0, chunks, lambda c: weight_copy(2, c).start())
-    acc[...] = jnp.zeros_like(acc)
+    acc_t[...] = jnp.zeros_like(acc_t)
 
     barrier = pltpu.get_barrier_semaphore()
     loop(1, groups, lambda k: pl.semaphore_signal(
@@ -263,18 +276,22 @@
     gather_forward(1)
     loop(early, chunks, gate_up)
     gather_finish(1)
-    tok_copy = pltpu.make_async_copy(tok, tok_out, full_sem.at[0])
     grad_copy = pltpu.make_async_copy(grad, grad_out, full_sem.at[1])
+    grad_copy.start()
+    grad_t[...] = grad[...].T
+    loop(0, chunks, down)
+    tok_t[...] = tok[...].T
+    tok_copy = pltpu.make_async_copy(tok_t, tok_out, full_sem.at[0])
     tok_copy.start()
-    grad_copy.start()
-    loop(0, chunks, down)
     chip_sum(2, chunks - 1)
     loop(0, chunks, finish)
     input_product(chunks - 1)
 
-    for k in range(n):
-        owner = lax.rem(me + k, n)
-        partial_outs[k][...] = acc[place(owner), :].astype(BF16)
+    acc[...] = acc_t[...].T
+    side = lax.rem(me, 2)
+    for k in range(n // 2):
+        keep_out[k] = acc[place(2 * k + side), :]
+        send_out[k] = acc[place(2 * k + 1 - side), :].astype(BF16)
 
     gather_drain(0)
     gather_drain(1)
@@ -297,22 +314,30 @@
     total = block * n
     width = chunk_width(units)
     chunks = units // width
-    group = 2 if n % 2 == 0 else 1
+    group = 2
     half = total // 2
     anywhere = pl.BlockSpec(memory_space=pl.ANY)
     inside = pl.BlockSpec(memory_space=pltpu.VMEM)
     full = jax.ShapeDtypeStruct((total, depth), BF16)
     hidden = jax.ShapeDtypeStruct((total, units), BF16)
-    piece = jax.ShapeDtypeStruct((block, depth), BF16)
+    turned = jax.ShapeDtypeStruct((depth, total), BF16)
+    hidden_t = jax.ShapeDtypeStruct((units, total), BF16)
     dma = pltpu.SemaphoreType.DMA
     return pl.pallas_call(
         functools.partial(forward_kernel, n, group, chunks, width),
-        out_shape=[full] * 2 + [hidden] * 3 + [piece] * n,
+        out_shape=[
+            turned, full, hidden_t, hidden, hidden,
+            jax.ShapeDtypeStruct((n // 2, block, depth), F32),
+            jax.ShapeDtypeStruct((n // 2, block, depth), BF16),
+        ],
         in_specs=[anywhere] * 5,
-        out_specs=[anywhere] * 5 + [inside] * n,
+        out_specs=[anywhere] * 5 + [inside] * 2,
         scratch_shapes=[
             pltpu.VMEM((total, depth), BF16),
             pltpu.VMEM((total, depth), BF16),
+            pltpu.VMEM((depth, total), BF16),
+            pltpu.VMEM((depth, total), BF16),
+            pltpu.VMEM((units, total), BF16),
             pltpu.VMEM((depth, units), BF16),
             pltpu.VMEM((depth, units), BF16),
             pltpu.VMEM((units, depth), BF16),
@@ -321,6 +346,8 @@
             pltpu.VMEM((3, chunks, half, width), BF16),
             pltpu.VMEM((3, chunks, half, width), BF16),
             pltpu.VMEM((chunks, 3, total, width), BF16),
+            pltpu.VMEM((2, width, total), BF16),
+            pltpu.VMEM((depth, total), F32),
             pltpu.VMEM((total, depth), F32),
             dma((3, chunks)),
             dma((2,)),
@@ -343,61 +370,62 @@
     )(tokens, out_grad, gate_w, up_w, down_w)
 
 
-def grads_kernel(tok, grad, hidden, d_gate, d_up, gate_o, up_o, down_o, tok_t, hid_t):
-    step = pl.program_id(0)
-
-    @pl.when(step == 0)
-    def _():
-        tok_t[...] = tok[...].T
-        hid_t[...] = hidden[...].T
-
-    rows = gate_o.shape[0]
-    left = tok_t[pl.ds(pl.multiple_of(step * rows, rows), rows), :]
-    gate_o[...] = jnp.dot(left, d_gate[...], preferred_element_type=F32).astype(BF16)
-    up_o[...] = jnp.dot(left, d_up[...], preferred_element_type=F32).astype(BF16)
-    units = down_o.shape[0]
-    left = hid_t[pl.ds(pl.multiple_of(step * units, units), units), :]
-    down_o[...] = jnp.dot(left, grad[...], preferred_element_type=F32).astype(BF16)
-
-
-def weight_grads(tok, grad, hidden, d_gate, d_up):
-    total, depth = tok.shape
-    units = hidden.shape[1]
-    steps = max(s for s in (1, 2, 4, 8) if depth % (16 * s) == 0 and units % (16 * s) == 0)
-    inside = pl.BlockSpec(memory_space=pltpu.VMEM)
-    wide = pl.BlockSpec((depth // steps, units), lambda i: (i, 0))
-    tall = pl.BlockSpec((units // steps, depth), lambda i: (i, 0))
+def grad_kernel(left, right, out):
+    out[...] = jnp.dot(left[...], right[...], preferred_element_type=F32).astype(BF16)
+
+
+def weight_grad(name, grant, left, right):
+    rows, total = left.shape
+    width = right.shape[1]
+    steps = max(s for s in (1, 2, 4, 8) if rows % (16 * s) == 0)
     return pl.pallas_call(
-        grads_kernel,
+        grad_kernel,
         grid=(steps,),
-        out_shape=[
-            jax.ShapeDtypeStruct((depth, units), BF16),
-            jax.ShapeDtypeStruct((depth, units), BF16),
-            jax.ShapeDtypeStruct((units, depth), BF16),
+        out_shape=jax.ShapeDtypeStruct((rows, width), BF16),
+        in_specs=[
+            pl.BlockSpec((rows // steps, total), lambda i: (i, 0)),
+            pl.BlockSpec((total, width), lambda i: (0, 0)),
         ],
-        in_specs=[inside] * 5,
-        out_specs=[wide, wide, tall],
-        scratch_shapes=[pltpu.VMEM((depth, total), BF16), pltpu.VMEM((units, total), BF16)],
-        compiler_params=pltpu.CompilerParams(vmem_limit_bytes=48 * 2**20),
+        out_specs=pl.BlockSpec((rows // steps, width), lambda i: (i, 0)),
+        compiler_params=pltpu.CompilerParams(vmem_limit_bytes=grant * 2**20),
         cost_estimate=pl.CostEstimate(
-            flops=6 * total * depth * units, bytes_accessed=6 * depth * units, transcendentals=0
+            flops=2 * total * rows * width, bytes_accessed=2 * rows * width, transcendentals=0
         ),
-        name="weight_grads",
-    )(tok, grad, hidden, d_gate, d_up)
+        name=name,
+    )(left, right)
 
 
 def local(n, tokens, out_grad, gate_weight, up_weight, down_weight):
-    tok, grad, hidden, d_gate, d_up, *pieces = forward(
+    tok_t, grad, hid_t, d_gate, d_up, keep, send = forward(
         n, tokens, out_grad, gate_weight, up_weight, down_weight
     )
-    arrived = [
-        lax.ppermute(pieces[k], "col", [(i, (i + k) % n) for i in range(n)]) for k in range(1, n)
-    ]
-    grad_gate, grad_up, grad_down = weight_grads(tok, grad, hidden, d_gate, d_up)
-    total = pieces[0].astype(F32)
-    for piece in arrived:
-        total = total + piece.astype(F32)
-    return total.astype(BF16), grad_gate, grad_up, grad_down
+    products = [("grad_gate", tok_t, d_gate), ("grad_up", tok_t, d_up), ("grad_down", hid_t, grad)]
+    results = []
+    me = lax.axis_index("col")
+    bit, left = 1, n // 2
+    while True:
+        arrived = lax.ppermute(send, "col", [(i, i ^ bit) for i in range(n)])
+        if products:
+            name, first, second = products.pop(0)
+            if results:
+                second, _ = lax.optimization_barrier((second, send))
+            results.append(weight_grad(name, 48 if results else 62, first, second))
+        bit *= 2
+        if left == 1:
+            break
+        left //= 2
+        pair = (left, 2) + keep.shape[1:]
+        side = (me // bit) % 2
+        halves = [
+            lax.dynamic_index_in_dim(keep.reshape(pair), s, 1, False)
+            + lax.dynamic_index_in_dim(arrived.reshape(pair), s, 1, False).astype(F32)
+            for s in (side, 1 - side)
+        ]
+        keep, send = halves[0], halves[1].astype(BF16)
+    for name, first, second in products:
+        results.append(weight_grad(name, 48, first, second))
+    total = keep[0] + arrived[0].astype(F32)
+    return (total.astype(BF16), *results)
 
 
 def solution(mesh):

time: 93.5 us -> 96.7 us (1.034)
  Pallas kernels: 74.9 us -> 86.8 us
  starting transfers between devices: 11.3 us -> 4.83 us
  local copies, waits for them, and re-layouts: 5.62 us -> 1.19 us
  other arithmetic: 0.7 us -> 2.7 us
    pallas_call x1 -> x3, Pallas kernels: 17.3 us -> 25.7 us  [weight_grad(): pl.pallas_call(grad_kernel, grid=(steps,), out_shape=jax.ShapeDtypeStruct...]
    ppermute x7 -> x3, starting transfers between devices: 11.3 us -> 4.83 us  [local(): arrived = lax.ppermute(send, 'col', [(i, i ^ bit) for i in range(n)])]
    unnamed x12 -> x8, local copies, waits for them, and re-layouts: 5.62 us -> 1.19 us
    pallas_call x1, Pallas kernels: 57.6 us -> 61.1 us  [forward(): pl.pallas_call(functools.partial(forward_kernel, n, group, chunks, width)...]
    add x0 -> x1, other arithmetic: none -> 1.02 us  [local(): lax.dynamic_index_in_dim(keep.reshape(pair), s, 1, False)]
    convert_element_type x1 -> x3, other arithmetic: 0.7 us -> 1.68 us  [the longest x2 1.03 us: local(): keep, send = (halves[0], halves[1].astype(BF16))]
  transfers between devices with their start and end apart: 7 -> 3, of which waited for: 0 -> 0; matrix products, arithmetic and copies ran while one was open for 0% -> 0% of each run, Pallas kernels for 19% -> 27%
where the time goes in v2:
time: 96.7 us; the launch traced here: 96.2 us
  Pallas kernels  86.8 us (90%)
  starting transfers between devices  4.83 us (5%)
  other arithmetic  2.7 us (3%)
  local copies, waits for them, and re-layouts  1.19 us (1%)
    pallas_call x1, Pallas kernels, forward(): pl.pallas_call(functools.partial(forward_kernel, n, group, chunks, width)...  61.1 us
    pallas_call x3, Pallas kernels, weight_grad(): pl.pallas_call(grad_kernel, grid=(steps,), out_shape=jax.ShapeDtypeStruct...  25.7 us
    ppermute x3, starting transfers between devices, local(): arrived = lax.ppermute(send, 'col', [(i, i ^ bit) for i in range(n)])  4.83 us
  transfers between devices with their start and end apart: 3, of which 0 were waited for; matrix products, arithmetic and copies ran while one was open for 0% of the time, Pallas kernels for 27%

profile of v2, /device:TPU:0, one launch (start us, length us, event | category | flops | bytes accessed | tf_op | source)
XLA Modules:
  0.0 96.2 jit_solution(1604643462562194574)
XLA Ops:
  0.6 61.1 %forward_exchange.1 = (bf16[2048,128]{1,0:T(8,128)(2,1)}, bf16[128,2048]{1,0:T(8,128)(2,1)}, bf16[3584,128]{1,0:T(8,128)(2,1)}, bf16[128,3584]{1,0:T(8,128)(2,1)...) custom-call(bf16[16,2048]{1,0:T(8,128)(2,1)} %tokens.1, ...), custom_call_target="tpu_custom_call" | custom-call | tf_op jit(solution)/shard_map/forward_exchange/pallas_call | solution.py:326
  61.8 0.0 copy-start
  61.8 0.6 collective-permute-start
  62.4 0.0 copy-start.1
  62.4 0.0 copy-start.3
  62.4 9.6 %grad_gate.1 = bf16[2048,3584]{1,0:T(8,128)(2,1)} custom-call(bf16[2048,128]{1,0:T(8,128)(2,1)} %get-tuple-element.15.left, bf16[128,3584]{1,0:T(8,128)(2,1)} %get-tuple-element.16.right), custom_call_target="tpu_custom_call" | custom-call | flops 1879048192 | bytes 14680064 | tf_op jit(solution)/shard_map/grad_gate/pallas_call | solution.py:381
  72.0 0.0 collective-permute-done
  72.0 1.0 %fusion.1 = bf16[2,16,2048]{2,1,0:T(8,128)(2,1)S(1)} fusion(f32[2,2,16,2048]{3,2,1,0:T(8,128)} %bitcast.26, s32[]{:T(128)S(6)} %select_n.44, bf16[2,2,16,2048]{3,2,1,0:T(8,128)(2,1)} %bitcast.1), kind=kLoop, calls=%fused_computation.3 | loop fusion | flops 196608 | bytes 524292 | tf_op jit(solution)/shard_map/convert_element_type | solution.py:424
  73.0 1.0 %convert_add_fusion = f32[2,1,16,2048]{3,2,1,0:T(8,128)S(1)} fusion(f32[2,2,16,2048]{3,2,1,0:T(8,128)} %bitcast.27, s32[]{:T(128)S(6)} %select_n.40, bf16[2,2,16,2048]{3,2,1,0:T(8,128)(2,1)} %bitcast.1), kind=kLoop, calls=%fused_computation.2 | loop fusion | flops 131072 | bytes 655364 | tf_op jit(solution)/shard_map/add | solution.py:420
  74.1 1.6 %collective-permute-start.1 = (bf16[2,16,2048]{2,1,0:T(8,128)(2,1)S(1)}, bf16[2,16,2048]{2,1,0:T(8,128)(2,1)S(1)}, u32[]{:S(2)}, u32[]{:S(2)}) collective-permute-start(bf16[2,16,2048]{2,1,0:T(8,128)(2,1)S(1)} %fusion.1), channel_id=1, source_target_pairs={{0,2},{1,3},{2,0},{3,1},{4,6},{5,7},{6,4},{7,5},{8,10},{9,11},{10,... | collective-permute-start | bytes 393224 | tf_op jit(solution)/shard_map/ppermute | solution.py:407
  75.6 0.0 copy-done
  75.6 0.0 copy-start.2
  75.6 1.2 %copy-done.2 = bf16[128,3584]{1,0:T(8,128)(2,1)S(1)} copy-done((bf16[128,3584]{1,0:T(8,128)(2,1)S(1)}, bf16[128,3584]{1,0:T(8,128)(2,1)}, u32[]{:S(2)}) %copy-start.2) | copy-done | bytes 917528
  76.8 8.0 %grad_up.1 = bf16[2048,3584]{1,0:T(8,128)(2,1)} custom-call(bf16[2048,128]{1,0:T(8,128)(2,1)S(1)} %copy-done, bf16[128,3584]{1,0:T(8,128)(2,1)S(1)} %copy-done.2), custom_call_target="tpu_custom_call" | custom-call | flops 1879048192 | bytes 14680064 | tf_op jit(solution)/shard_map/grad_up/pallas_call | solution.py:381
  84.9 0.0 collective-permute-done.1
  84.9 2.6 %collective-permute-start.2 = (bf16[1,16,2048]{2,1,0:T(8,128)(2,1)S(1)}, bf16[1,16,2048]{2,1,0:T(8,128)(2,1)S(1)}, u32[]{:S(2)}, u32[]{:S(2)}) collective-permute-start(bf16[1,16,2048]{2,1,0:T(8,128)(2,1)S(1)} %fusion.2), channel_id=1, source_target_pairs={{0,4},{1,5},{2,6},{3,7},{4,0},{5,1},{6,2},{7,3},{8,12},{9,13},{10,... | collective-permute-start | bytes 196616 | tf_op jit(solution)/shard_map/ppermute | solution.py:407
  87.5 0.0 copy-done.1
  87.5 0.0 copy-done.3
  87.5 8.0 %grad_down.1 = bf16[3584,2048]{1,0:T(8,128)(2,1)} custom-call(bf16[3584,128]{1,0:T(8,128)(2,1)S(1)} %copy-done.1, bf16[128,2048]{1,0:T(8,128)(2,1)S(1)} %copy-done.3), custom_call_target="tpu_custom_call" | custom-call | flops 1879048192 | bytes 14680064 | tf_op jit(solution)/shard_map/grad_down/pallas_call | solution.py:381
  95.6 0.0 collective-permute-done.2
  95.6 0.7 fusion.5
  (1 shorter events, 0.0 us)
Async XLA Ops:
  61.8 13.9 %copy-start = (bf16[2048,128]{1,0:T(8,128)(2,1)S(1)}, bf16[2048,128]{1,0:T(8,128)(2,1)}, u32[]{:S(2)}) copy-start(bf16[2048,128]{1,0:T(8,128)(2,1)} %get-tuple-element.15.left) | copy-start | bytes 1572868
  61.8 10.2 %collective-permute-start = (bf16[4,16,2048]{2,1,0:T(8,128)(2,1)}, bf16[4,16,2048]{2,1,0:T(8,128)(2,1)}, u32[]{:S(2)}, u32[]{:S(2)}) collective-permute-start(bf16[4,16,2048]{2,1,0:T(8,128)(2,1)} %get-tuple-element.14), channel_id=1, source_target_pairs={{0,1},{1,0},{2,3},{3,2},{4,5},{5,4},{6,7},{7,6},{8,9},{9,8},{10,11... | collective-permute-start | bytes 786440 | tf_op jit(solution)/shard_map/ppermute | solution.py:407
  62.4 25.1 %copy-start.1 = (bf16[3584,128]{1,0:T(8,128)(2,1)S(1)}, bf16[3584,128]{1,0:T(8,128)(2,1)}, u32[]{:S(2)}) copy-start(bf16[3584,128]{1,0:T(8,128)(2,1)} %get-tuple-element.19.left) | copy-start | bytes 2752516
  62.4 25.1 %copy-start.3 = (bf16[128,2048]{1,0:T(8,128)(2,1)S(1)}, bf16[128,2048]{1,0:T(8,128)(2,1)}, u32[]{:S(2)}) copy-start(bf16[128,2048]{1,0:T(8,128)(2,1)} %get-tuple-element.21.right) | copy-start | bytes 1572868
  74.1 10.8 %collective-permute-start.1 = (bf16[2,16,2048]{2,1,0:T(8,128)(2,1)S(1)}, bf16[2,16,2048]{2,1,0:T(8,128)(2,1)S(1)}, u32[]{:S(2)}, u32[]{:S(2)}) collective-permute-start(bf16[2,16,2048]{2,1,0:T(8,128)(2,1)S(1)} %fusion.1), channel_id=1, source_target_pairs={{0,2},{1,3},{2,0},{3,1},{4,6},{5,7},{6,4},{7,5},{8,10},{9,11},{10,... | collective-permute-start | bytes 393224 | tf_op jit(solution)/shard_map/ppermute | solution.py:407
  75.6 1.2 %copy-start.2 = (bf16[128,3584]{1,0:T(8,128)(2,1)S(1)}, bf16[128,3584]{1,0:T(8,128)(2,1)}, u32[]{:S(2)}) copy-start(bf16[128,3584]{1,0:T(8,128)(2,1)} %get-tuple-element.18.right) | copy-start | bytes 2752516
  84.9 10.7 %collective-permute-start.2 = (bf16[1,16,2048]{2,1,0:T(8,128)(2,1)S(1)}, bf16[1,16,2048]{2,1,0:T(8,128)(2,1)S(1)}, u32[]{:S(2)}, u32[]{:S(2)}) collective-permute-start(bf16[1,16,2048]{2,1,0:T(8,128)(2,1)S(1)} %fusion.2), channel_id=1, source_target_pairs={{0,4},{1,5},{2,6},{3,7},{4,0},{5,1},{6,2},{7,3},{8,12},{9,13},{10,... | collective-permute-start | bytes 196616 | tf_op jit(solution)/shard_map/ppermute | solution.py:407

commit v3 on v1

--- a/solution.py
+++ b/solution.py
@@ -42,15 +42,15 @@
 def forward_kernel(
     n, group, chunks, width,
     tokens, out_grad, gate_w, up_w, down_w,
-    tok_out, grad_out, hid_out, dgate_out, dup_out, *rest,
+    tok_out, grad_out, hid_out, dgate_out, dup_out, pieces_out,
+    *scratch,
 ):
-    partial_outs = rest[:n]
     (
-        tok, grad, wg, wu, wd, part, core_in, x_send, x_in, res, acc,
+        tok, grad, tok_t, hid_t, wg, wu, wd, part, core_in, x_send, x_in, res, acc,
         w_sem, own_sem, ag_send, ag_fwd, ag_recv,
         core_send_sem, core_recv_sem, x_send_sem, x_recv_sem, res_send_sem, res_recv_sem,
         out_sem, full_sem,
-    ) = rest[n:]
+    ) = scratch
     block = tokens.shape[0]
     total = block * n
     half = total // 2
@@ -182,7 +182,11 @@
         )
 
     def out_copy(k, c):
-        target = (hid_out, dgate_out, dup_out)[k]
+        if k == 0:
+            return pltpu.make_async_copy(
+                hid_t.at[columns(c), :], hid_out.at[columns(c), :], out_sem.at[k, c]
+            )
+        target = (dgate_out, dup_out)[k - 1]
         return pltpu.make_async_copy(res.at[c, k], target.at[:, columns(c)], out_sem.at[k, c])
 
     def multiply(m, c):
@@ -203,29 +207,36 @@
 
     def gate_up(c):
         multiply(0, c)
-        multiply(1, c)
 
         @pl.when(c > 0)
         def _():
-            chip_sum(0, c - 1)
             chip_sum(1, c - 1)
+
+        multiply(1, c)
+        chip_sum(0, c)
 
     def down(c):
         multiply(2, c)
-
-        @pl.when(c == 0)
-        def _():
-            chip_sum(0, chunks - 1)
-            chip_sum(1, chunks - 1)
 
         @pl.when(c > 0)
         def _():
             chip_sum(2, c - 1)
 
+    def later(c):
+        multiply(0, c)
+        multiply(1, c)
+        chip_sum(0, c)
+        multiply(2, c)
+        chip_sum(1, c)
+        finish(c - early)
+        chip_sum(2, c)
+
     def input_product(c):
         res_copy(c).wait_recv()
-        for k in range(3):
-            out_copy(k, c).start()
+        out_copy(1, c).start()
+        out_copy(2, c).start()
+        hid_t[columns(c), :] = res[c, 0].T
+        out_copy(0, c).start()
         acc[...] += contract_last(res[c, 1], wg[:, columns(c)])
         acc[...] += contract_last(res[c, 2], wu[:, columns(c)])
 
@@ -260,21 +271,22 @@
     gather_finish(0)
     early = min(3, chunks)
     loop(0, early, gate_up)
+    chip_sum(1, early - 1)
     gather_forward(1)
-    loop(early, chunks, gate_up)
+    tok_t[...] = tok[...].T
+    tok_copy = pltpu.make_async_copy(tok_t, tok_out, full_sem.at[0])
+    tok_copy.start()
     gather_finish(1)
-    tok_copy = pltpu.make_async_copy(tok, tok_out, full_sem.at[0])
     grad_copy = pltpu.make_async_copy(grad, grad_out, full_sem.at[1])
-    tok_copy.start()
     grad_copy.start()
-    loop(0, chunks, down)
-    chip_sum(2, chunks - 1)
-    loop(0, chunks, finish)
+    loop(0, early, down)
+    chip_sum(2, early - 1)
+    loop(early, chunks, later)
+    loop(chunks - early, chunks, finish)
     input_product(chunks - 1)
 
     for k in range(n):
-        owner = lax.rem(me + k, n)
-        partial_outs[k][...] = acc[place(owner), :].astype(BF16)
+        pieces_out[k] = acc[k * block : (k + 1) * block, :].astype(BF16)
 
     gather_drain(0)
     gather_drain(1)
@@ -297,22 +309,28 @@
     total = block * n
     width = chunk_width(units)
     chunks = units // width
-    group = 2 if n % 2 == 0 else 1
+    group = 2
     half = total // 2
     anywhere = pl.BlockSpec(memory_space=pl.ANY)
     inside = pl.BlockSpec(memory_space=pltpu.VMEM)
     full = jax.ShapeDtypeStruct((total, depth), BF16)
     hidden = jax.ShapeDtypeStruct((total, units), BF16)
-    piece = jax.ShapeDtypeStruct((block, depth), BF16)
+    turned = jax.ShapeDtypeStruct((depth, total), BF16)
+    hidden_t = jax.ShapeDtypeStruct((units, total), BF16)
     dma = pltpu.SemaphoreType.DMA
     return pl.pallas_call(
         functools.partial(forward_kernel, n, group, chunks, width),
-        out_shape=[full] * 2 + [hidden] * 3 + [piece] * n,
+        out_shape=[
+            turned, full, hidden_t, hidden, hidden,
+            jax.ShapeDtypeStruct((n, block, depth), BF16),
+        ],
         in_specs=[anywhere] * 5,
-        out_specs=[anywhere] * 5 + [inside] * n,
+        out_specs=[anywhere] * 5 + [inside],
         scratch_shapes=[
             pltpu.VMEM((total, depth), BF16),
             pltpu.VMEM((total, depth), BF16),
+            pltpu.VMEM((depth, total), BF16),
+            pltpu.VMEM((units, total), BF16),
             pltpu.VMEM((depth, units), BF16),
             pltpu.VMEM((depth, units), BF16),
             pltpu.VMEM((units, depth), BF16),
@@ -343,30 +361,24 @@
     )(tokens, out_grad, gate_w, up_w, down_w)
 
 
-def grads_kernel(tok, grad, hidden, d_gate, d_up, gate_o, up_o, down_o, tok_t, hid_t):
-    step = pl.program_id(0)
-
-    @pl.when(step == 0)
-    def _():
-        tok_t[...] = tok[...].T
-        hid_t[...] = hidden[...].T
-
-    rows = gate_o.shape[0]
-    left = tok_t[pl.ds(pl.multiple_of(step * rows, rows), rows), :]
-    gate_o[...] = jnp.dot(left, d_gate[...], preferred_element_type=F32).astype(BF16)
-    up_o[...] = jnp.dot(left, d_up[...], preferred_element_type=F32).astype(BF16)
-    units = down_o.shape[0]
-    left = hid_t[pl.ds(pl.multiple_of(step * units, units), units), :]
-    down_o[...] = jnp.dot(left, grad[...], preferred_element_type=F32).astype(BF16)
-
-
-def weight_grads(tok, grad, hidden, d_gate, d_up):
-    total, depth = tok.shape
-    units = hidden.shape[1]
+def grads_kernel(tok_t, hid_t, d_gate, d_up, grad, gate_o, up_o, down_o):
+    for left, right, out in (
+        (tok_t, d_gate, gate_o), (tok_t, d_up, up_o), (hid_t, grad, down_o)
+    ):
+        out[...] = jnp.dot(left[...], right[...], preferred_element_type=F32).astype(BF16)
+
+
+def weight_grads(tok_t, hid_t, d_gate, d_up, grad):
+    depth, total = tok_t.shape
+    units = hid_t.shape[0]
     steps = max(s for s in (1, 2, 4, 8) if depth % (16 * s) == 0 and units % (16 * s) == 0)
-    inside = pl.BlockSpec(memory_space=pltpu.VMEM)
-    wide = pl.BlockSpec((depth // steps, units), lambda i: (i, 0))
-    tall = pl.BlockSpec((units // steps, depth), lambda i: (i, 0))
+
+    def rows(count, width):
+        return pl.BlockSpec((count // steps, width), lambda i: (i, 0))
+
+    def whole(array):
+        return pl.BlockSpec(array.shape, lambda i: (0, 0))
+
     return pl.pallas_call(
         grads_kernel,
         grid=(steps,),
@@ -375,29 +387,26 @@
             jax.ShapeDtypeStruct((depth, units), BF16),
             jax.ShapeDtypeStruct((units, depth), BF16),
         ],
-        in_specs=[inside] * 5,
-        out_specs=[wide, wide, tall],
-        scratch_shapes=[pltpu.VMEM((depth, total), BF16), pltpu.VMEM((units, total), BF16)],
-        compiler_params=pltpu.CompilerParams(vmem_limit_bytes=48 * 2**20),
+        in_specs=[rows(depth, total), rows(units, total), whole(d_gate), whole(d_up), whole(grad)],
+        out_specs=[rows(depth, units), rows(depth, units), rows(units, depth)],
+        compiler_params=pltpu.CompilerParams(vmem_limit_bytes=62 * 2**20),
         cost_estimate=pl.CostEstimate(
             flops=6 * total * depth * units, bytes_accessed=6 * depth * units, transcendentals=0
         ),
         name="weight_grads",
-    )(tok, grad, hidden, d_gate, d_up)
+    )(tok_t, hid_t, d_gate, d_up, grad)
 
 
 def local(n, tokens, out_grad, gate_weight, up_weight, down_weight):
-    tok, grad, hidden, d_gate, d_up, *pieces = forward(
+    tok_t, grad, hid_t, d_gate, d_up, pieces = forward(
         n, tokens, out_grad, gate_weight, up_weight, down_weight
     )
-    arrived = [
-        lax.ppermute(pieces[k], "col", [(i, (i + k) % n) for i in range(n)]) for k in range(1, n)
-    ]
-    grad_gate, grad_up, grad_down = weight_grads(tok, grad, hidden, d_gate, d_up)
-    total = pieces[0].astype(F32)
-    for piece in arrived:
-        total = total + piece.astype(F32)
-    return total.astype(BF16), grad_gate, grad_up, grad_down
+    arrived = lax.all_to_all(pieces, "col", 0, 0, tiled=True)
+    grad_gate, grad_up, grad_down = weight_grads(tok_t, hid_t, d_gate, d_up, grad)
+    grad_input = arrived[0].astype(F32)
+    for k in range(1, n):
+        grad_input = grad_input + arrived[k].astype(F32)
+    return grad_input.astype(BF16), grad_gate, grad_up, grad_down
 
 
 def solution(mesh):

time: 93.5 us -> 82 us (0.88)
  starting transfers between devices: 11.3 us -> 4.85 us
  local copies, waits for them, and re-layouts: 5.62 us -> 0 us
    ppermute x7 -> x0, starting transfers between devices: 11.3 us -> none  [local(): lax.ppermute(pieces[k], 'col', [(i, (i + k) % n) for i in range(n)])]
    unnamed x12 -> x0, local copies, waits for them, and re-layouts: 5.62 us -> none
    all_to_all x0 -> x1, starting transfers between devices: none -> 4.85 us  [local(): arrived = lax.all_to_all(pieces, 'col', 0, 0, tiled=True)]
    pallas_call x1, Pallas kernels: 57.6 us -> 59.2 us  [forward(): pl.pallas_call(functools.partial(forward_kernel, n, group, chunks, width)...]
  transfers between devices with their start and end apart: 7 -> 1, of which waited for: 0 -> 0; matrix products, arithmetic and copies ran while one was open for 0% -> 0% of each run, Pallas kernels for 19% -> 20%
where the time goes in v3:
time: 82 us; the launch traced here: 81.8 us
  Pallas kernels  75.6 us (92%)
  starting transfers between devices  4.85 us (6%)
    pallas_call x1, Pallas kernels, forward(): pl.pallas_call(functools.partial(forward_kernel, n, group, chunks, width)...  59.2 us
    pallas_call x1, Pallas kernels, weight_grads(): pl.pallas_call(grads_kernel, grid=(steps,), out_shape=[jax.ShapeDtypeStru...  16.4 us
    all_to_all x1, starting transfers between devices, local(): arrived = lax.all_to_all(pieces, 'col', 0, 0, tiled=True)  4.85 us
  transfers between devices with their start and end apart: 1, of which 0 were waited for; matrix products, arithmetic and copies ran while one was open for 0% of the time, Pallas kernels for 20%

profile of v3, /device:TPU:0, one launch (start us, length us, event | category | flops | bytes accessed | tf_op | source)
XLA Modules:
  0.0 81.8 jit_solution(10219943299774736953)
XLA Ops:
  0.6 59.2 %forward_exchange.1 = (bf16[2048,128]{1,0:T(8,128)(2,1)}, bf16[128,2048]{1,0:T(8,128)(2,1)}, bf16[3584,128]{1,0:T(8,128)(2,1)}, bf16[128,3584]{1,0:T(8,128)(2,1)...) custom-call(bf16[16,2048]{1,0:T(8,128)(2,1)} %tokens.1, bf16[16,2048]{1,0:T(8,128)(2,1)} %out_grad.1, ...), custom_call_target="tpu_custom_call" | custom-call | tf_op jit(solution)/shard_map/forward_exchange/pallas_call | solution.py:321
  59.9 4.9 %all-to-all-start = ((bf16[8,16,2048]{2,1,0:T(8,128)(2,1)}), bf16[8,16,2048]{2,1,0:T(8,128)(2,1)S(1)}, u32[]{:S(2)}, u32[]{:S(2)}) async-start(bf16[8,16,2048]{2,1,0:T(8,128)(2,1)} %get-tuple-element.13), calls=%async_computation | async-start | bytes 1048576 | tf_op jit(solution)/shard_map/all_to_all | solution.py:404
  64.7 16.4 %weight_grads.1 = (bf16[2048,3584]{1,0:T(8,128)(2,1)}, bf16[2048,3584]{1,0:T(8,128)(2,1)}, bf16[3584,2048]{1,0:T(8,128)(2,1)}) custom-call(bf16[2048,128]{1,0:T(8,128)(2,1)} %get-tuple-element.14.tok_t, bf16[3584,128]{1,0:T(8,128)(2,1)} %get-tuple-element.15.hid_t, bf16[128,3584]{1,0:T(8,128)(2,1)} %get-tuple-element.16.d_gate, ...), custom_call_target="tpu_custom_call" | custom-call | flops 5637144576 | bytes 44040192 | tf_op jit(solution)/shard_map/weight_grads/pallas_call | solution.py:382
  81.1 0.0 all-to-all-done
  81.1 0.7 fusion
Async XLA Ops:
  59.9 21.3 %all-to-all-start = ((bf16[8,16,2048]{2,1,0:T(8,128)(2,1)}), bf16[8,16,2048]{2,1,0:T(8,128)(2,1)S(1)}, u32[]{:S(2)}, u32[]{:S(2)}) async-start(bf16[8,16,2048]{2,1,0:T(8,128)(2,1)} %get-tuple-element.13), calls=%async_computation | async-start | bytes 1048576 | tf_op jit(solution)/shard_map/all_to_all | solution.py:404

commit v4 on v3

--- a/solution.py
+++ b/solution.py
@@ -206,14 +206,12 @@
         x_copy(m, c).start()
 
     def gate_up(c):
-        multiply(0, c)
-
-        @pl.when(c > 0)
-        def _():
-            chip_sum(1, c - 1)
-
-        multiply(1, c)
-        chip_sum(0, c)
+        for m in range(2):
+            multiply(m, c)
+
+            @pl.when(c > 0)
+            def _():
+                chip_sum(m, c - 1)
 
     def down(c):
         multiply(2, c)
@@ -224,12 +222,16 @@
 
     def later(c):
         multiply(0, c)
+
+        @pl.when(c > early)
+        def _():
+            chip_sum(1, c - 1)
+
         multiply(1, c)
+        chip_sum(2, c - 1)
+        multiply(2, c)
         chip_sum(0, c)
-        multiply(2, c)
-        chip_sum(1, c)
         finish(c - early)
-        chip_sum(2, c)
 
     def input_product(c):
         res_copy(c).wait_recv()
@@ -271,17 +273,20 @@
     gather_finish(0)
     early = min(3, chunks)
     loop(0, early, gate_up)
+    tok_t[...] = tok[...].T
+    chip_sum(0, early - 1)
     chip_sum(1, early - 1)
     gather_forward(1)
-    tok_t[...] = tok[...].T
     tok_copy = pltpu.make_async_copy(tok_t, tok_out, full_sem.at[0])
     tok_copy.start()
     gather_finish(1)
     grad_copy = pltpu.make_async_copy(grad, grad_out, full_sem.at[1])
     grad_copy.start()
     loop(0, early, down)
-    chip_sum(2, early - 1)
     loop(early, chunks, later)
+    if chunks > early:
+        chip_sum(1, chunks - 1)
+    chip_sum(2, chunks - 1)
     loop(chunks - early, chunks, finish)
     input_product(chunks - 1)
 

time: 82 us -> 80.8 us (0.985)
  Pallas kernels: 75.6 us -> 74.4 us
    pallas_call x1, Pallas kernels: 59.2 us -> 58 us  [forward(): pl.pallas_call(functools.partial(forward_kernel, n, group, chunks, width)...]
where the time goes in v4:
time: 80.8 us; the launch traced here: 80.6 us
  Pallas kernels  74.4 us (92%)
  starting transfers between devices  4.86 us (6%)
    pallas_call x1, Pallas kernels, forward(): pl.pallas_call(functools.partial(forward_kernel, n, group, chunks, width)...  58 us
    pallas_call x1, Pallas kernels, weight_grads(): pl.pallas_call(grads_kernel, grid=(steps,), out_shape=[jax.ShapeDtypeStru...  16.4 us
    all_to_all x1, starting transfers between devices, local(): arrived = lax.all_to_all(pieces, 'col', 0, 0, tiled=True)  4.86 us
  transfers between devices with their start and end apart: 1, of which 0 were waited for; matrix products, arithmetic and copies ran while one was open for 0% of the time, Pallas kernels for 20%

profile of v4, /device:TPU:0, one launch (start us, length us, event | category | flops | bytes accessed | tf_op | source)
XLA Modules:
  0.0 80.6 jit_solution(5407976410825041117)
XLA Ops:
  0.6 58.0 %forward_exchange.1 = (bf16[2048,128]{1,0:T(8,128)(2,1)}, bf16[128,2048]{1,0:T(8,128)(2,1)}, bf16[3584,128]{1,0:T(8,128)(2,1)}, bf16[128,3584]{1,0:T(8,128)(2,1)...) custom-call(bf16[16,2048]{1,0:T(8,128)(2,1)} %tokens.1, bf16[16,2048]{1,0:T(8,128)(2,1)} %out_grad.1, ...), custom_call_target="tpu_custom_call" | custom-call | tf_op jit(solution)/shard_map/forward_exchange/pallas_call | solution.py:326
  58.6 4.9 %all-to-all-start = ((bf16[8,16,2048]{2,1,0:T(8,128)(2,1)}), bf16[8,16,2048]{2,1,0:T(8,128)(2,1)S(1)}, u32[]{:S(2)}, u32[]{:S(2)}) async-start(bf16[8,16,2048]{2,1,0:T(8,128)(2,1)} %get-tuple-element.13), calls=%async_computation | async-start | bytes 1048576 | tf_op jit(solution)/shard_map/all_to_all | solution.py:409
  63.5 16.4 %weight_grads.1 = (bf16[2048,3584]{1,0:T(8,128)(2,1)}, bf16[2048,3584]{1,0:T(8,128)(2,1)}, bf16[3584,2048]{1,0:T(8,128)(2,1)}) custom-call(bf16[2048,128]{1,0:T(8,128)(2,1)} %get-tuple-element.14.tok_t, bf16[3584,128]{1,0:T(8,128)(2,1)} %get-tuple-element.15.hid_t, bf16[128,3584]{1,0:T(8,128)(2,1)} %get-tuple-element.16.d_gate, ...), custom_call_target="tpu_custom_call" | custom-call | flops 5637144576 | bytes 44040192 | tf_op jit(solution)/shard_map/weight_grads/pallas_call | solution.py:387
  79.9 0.0 all-to-all-done
  79.9 0.7 fusion
Async XLA Ops:
  58.6 21.3 %all-to-all-start = ((bf16[8,16,2048]{2,1,0:T(8,128)(2,1)}), bf16[8,16,2048]{2,1,0:T(8,128)(2,1)S(1)}, u32[]{:S(2)}, u32[]{:S(2)}) async-start(bf16[8,16,2048]{2,1,0:T(8,128)(2,1)} %get-tuple-element.13), calls=%async_computation | async-start | bytes 1048576 | tf_op jit(solution)/shard_map/all_to_all | solution.py:409
